TPU v7x, 512 devices: a whole 4x8x8 slice. The times are simulated.
512 devices in a mesh: section: 16 (over y, z_hi), dp: 16 (over z_lo, x), cores: 2 (over core).
Axes of the slice: x: 4, y: 8, z: 8 (z_hi: 2, z_lo: 4; z = z_hi * 4 + z_lo), core: 2. Of those that a mesh axis runs over, the one named last changes fastest.
Arguments:
- arrivals: bfloat16 [2, 1536, 2048], P(None, 'dp'), may hold values from -6 to 6
- in_flight: bfloat16 [16, 1536, 2048], P('section', 'dp'), may hold values from -6 to 6
- cotangent: bfloat16 [2, 1536, 2048], P(None, 'dp'), may hold values from -6 to 6
- grad_flight: bfloat16 [16, 1536, 2048], P('section', 'dp'), may hold values from -6 to 6
- stashed: bfloat16 [16, 2, 1536, 2048], P('section', None, 'dp'), may hold values from -6 to 6
- in_weight: bfloat16 [16, 2048, 4096], P('section', 'dp', 'cores'), may hold values from -0.125 to 0.125
- out_weight: bfloat16 [16, 1024, 2048], P('section', 'cores', 'dp'), may hold values from -0.1875 to 0.1875
- forward_blocks: int32 [16, 17], P('dp'), may hold values from 1 to 4, 42 in all within a row
- backward_blocks: int32 [16, 17], P('dp'), may hold values from 1 to 4, 42 in all within a row
- forward_marks: int32 [16, 17, 4, 4], P('dp'), may hold values 0 or 1
- backward_marks: int32 [16, 17, 4, 4], P('dp'), may hold values 0 or 1
Outputs:
- activations: bfloat16 [16, 2, 1536, 2048], P('section', None, ('dp', 'cores'))
- input_grads: bfloat16 [16, 2, 1536, 2048], P('section', None, ('dp', 'cores'))
- weight_grads: float32 [16, 1024, 2048], P('section', 'cores', 'dp')
Inputs may be any that keep to these rules, and one draw needn't show every extreme that they name: `forward_blocks`: in each replica's row the 17 lengths add up to 42 blocks and the longest is 4. `backward_blocks`: in each replica's row the 17 lengths add up to 42 blocks and the longest is 4.
All inputs are finite; a program needn't handle non-finite values. No bound on the sum of `forward_marks` or of `backward_marks` on one device may be relied on, other than what follows from the above.
Results may differ from a plain program's by a relative error of at most 0.03.
Values may be sent and summed in bfloat16 or wider, within the bound.
A program may use at most 64 MiB of HBM per device.

v0:
```python
import jax
import jax.numpy as jnp
from jax import lax
from jax.sharding import PartitionSpec as P

HEAD_DIM = 128
BLOCK = 24
BLOCKS = 4


EPSILON = 1e-06


def from_behind(x, axis, by):
    peers = lax.axis_size(axis)
    pairs = [(i, i + by) for i in range(peers) if 0 <= i + by < peers]
    return lax.ppermute(x, axis, pairs)


def block_keep(live_blocks, block_marks):
    length = BLOCKS * BLOCK
    places = jnp.arange(length, dtype=jnp.int32)
    owners = places // BLOCK
    onehot = (owners[:, None] == jnp.arange(BLOCKS, dtype=jnp.int32)[None, :]).astype(jnp.float32)
    spread = jnp.einsum("ia,rab,jb->rij", onehot, block_marks.astype(jnp.float32), onehot)
    allowed = (owners[:, None] == owners[None, :])[None] | (spread > 0.5)
    causal = (places[:, None] >= places[None, :])[None]
    tokens_live = live_blocks * BLOCK
    living = places[None, :] < tokens_live[:, None]
    keeping = causal & allowed & living[:, :, None] & living[:, None, :]
    return (keeping.astype(jnp.float32), 1.0 / tokens_live.astype(jnp.float32))


def choose_history(block_table, mark_table, history):
    histories = block_table.shape[1]
    matches = jnp.arange(histories, dtype=jnp.int32) == history
    blocks = jnp.sum(jnp.where(matches, block_table[0], 0))
    marked = jnp.sum(jnp.where(matches[:, None, None], mark_table[0], 0), axis=0)
    return block_keep(blocks[None], marked[None])


def norm_rows(values_f):
    return lax.rsqrt(jnp.mean(values_f * values_f, axis=-1, keepdims=True) + EPSILON)


def heads_forward(pre_act, keeping, inverse_count):
    scaling = HEAD_DIM ** (-0.5)
    active = jax.nn.silu(pre_act)
    gate_rows = active[:, :, :, 0]
    value_rows = active[:, :, :, 1].astype(jnp.bfloat16)
    query_rows = active[:, :, :, 2].astype(jnp.bfloat16)
    key_rows = active[:, :, :, 3].astype(jnp.bfloat16)
    scores = (
        jnp.einsum("rigd,rjgd->rgij", query_rows, key_rows, preferred_element_type=jnp.float32)
        * scaling
    )
    weights = keeping[:, None] * inverse_count[:, None, None, None]
    attention = (jax.nn.silu(scores) * weights).astype(jnp.bfloat16)
    mixed = jnp.einsum("rgij,rjgd->rigd", attention, value_rows, preferred_element_type=jnp.float32)
    root_scale = lax.rsqrt(jnp.mean(mixed * mixed, axis=-1, keepdims=True) + EPSILON)
    normed = mixed * root_scale
    gated = (normed * gate_rows).astype(jnp.bfloat16)
    return (
        gated,
        (
            gate_rows,
            value_rows,
            query_rows,
            key_rows,
            scores,
            weights,
            attention,
            root_scale,
            normed,
        ),
    )


def heads_backward(pre_act, saved, upstream):
    gate_rows, value_rows, query_rows, key_rows, scores, weights, attention, root_scale, normed = (
        saved
    )
    scaling = HEAD_DIM ** (-0.5)
    grad_gated = upstream.astype(jnp.float32)
    grad_normed = grad_gated * gate_rows
    grad_gate = grad_gated * normed
    grad_mixed = root_scale * (
        grad_normed - normed * jnp.mean(grad_normed * normed, axis=-1, keepdims=True)
    )
    mixed_low = grad_mixed.astype(jnp.bfloat16)
    grad_attention = jnp.einsum(
        "rigd,rjgd->rgij", mixed_low, value_rows, preferred_element_type=jnp.float32
    )
    grad_value = jnp.einsum(
        "rgij,rigd->rjgd", attention, mixed_low, preferred_element_type=jnp.float32
    )
    sigmoid_s = jax.nn.sigmoid(scores)
    grad_scores = (
        grad_attention * weights * sigmoid_s * (1.0 + scores * (1.0 - sigmoid_s)) * scaling
    ).astype(jnp.bfloat16)
    grad_query = jnp.einsum(
        "rgij,rjgd->rigd", grad_scores, key_rows, preferred_element_type=jnp.float32
    )
    grad_key = jnp.einsum(
        "rgij,rigd->rjgd", grad_scores, query_rows, preferred_element_type=jnp.float32
    )
    grad_active = jnp.stack([grad_gate, grad_value, grad_query, grad_key], axis=3)
    sigmoid_u = jax.nn.sigmoid(pre_act)
    return (grad_active * sigmoid_u * (1.0 + pre_act * (1.0 - sigmoid_u))).astype(jnp.bfloat16)


def per_device(
    arrivals,
    in_flight,
    cotangent,
    grad_flight,
    stashed,
    in_weight,
    out_weight,
    forward_blocks,
    backward_blocks,
    forward_marks,
    backward_marks,
):
    section_no = lax.axis_index("section")
    sections = lax.axis_size("section")
    core_no = lax.axis_index("cores")
    ticks = arrivals.shape[0]
    length = arrivals.shape[1]
    share = length // lax.axis_size("cores")
    row_start = core_no * share
    out_full = lax.all_gather(out_weight[0], "dp", axis=1, tiled=True)
    slab_rows = out_full.shape[0]
    groups = slab_rows // HEAD_DIM
    columns = in_weight.shape[2]
    in_full = None
    in_full = lax.all_gather(in_weight[0], "dp", axis=0, tiled=True)
    received = in_flight[0]
    returned = grad_flight[0]
    ahead_out = []
    back_out = []
    gated_list = []
    upstream_list = []
    for tick_no in range(ticks):
        if tick_no == 0:
            prior = in_flight[0]
            later = grad_flight[0]
        else:
            prior = received
            later = returned
        inputs = jnp.where(section_no == 0, arrivals[tick_no], prior)
        upstream = jnp.where(section_no == sections - 1, cotangent[tick_no], later)
        keep_ahead, count_ahead = choose_history(
            forward_blocks, forward_marks, tick_no - section_no + sections - 1
        )
        keep_back, count_back = choose_history(
            backward_blocks, backward_marks, tick_no + section_no
        )
        floats = inputs.astype(jnp.float32)
        saved_floats = stashed[0, tick_no].astype(jnp.float32)
        root_saved = norm_rows(saved_floats)
        scaled_saved = saved_floats * root_saved
        both_normed = jnp.concatenate(
            [(floats * norm_rows(floats)).astype(jnp.bfloat16), scaled_saved.astype(jnp.bfloat16)],
            axis=0,
        )
        pre_both = jnp.dot(both_normed, in_full, preferred_element_type=jnp.float32)
        pre_ahead = pre_both[:length].reshape(1, length, groups, 4, HEAD_DIM)
        pre_back = pre_both[length:].reshape(1, length, groups, 4, HEAD_DIM)
        gated_ahead, unused = heads_forward(pre_ahead, keep_ahead, count_ahead)
        partial_sum = jnp.dot(
            gated_ahead.reshape(length, slab_rows), out_full, preferred_element_type=jnp.float32
        )
        summed = lax.psum(partial_sum.astype(jnp.bfloat16), "cores").astype(jnp.float32)
        outgoing = (floats + summed).astype(jnp.bfloat16)
        ahead_out.append(lax.dynamic_slice_in_dim(outgoing, row_start, share, 0))
        if tick_no + 1 < ticks:
            received = from_behind(outgoing, "section", 1)
        gated_back, saved = heads_forward(pre_back, keep_back, count_back)
        grad_gated = (
            jnp.einsum("sd,fd->sf", upstream, out_full, preferred_element_type=jnp.float32)
            .astype(jnp.bfloat16)
            .reshape(1, length, groups, HEAD_DIM)
        )
        grad_pre = heads_backward(pre_back, saved, grad_gated).reshape(length, columns)
        grad_normed = jnp.einsum("sf,df->sd", grad_pre, in_full, preferred_element_type=jnp.float32)
        back_part = root_saved * (
            grad_normed
            - scaled_saved * jnp.mean(grad_normed * scaled_saved, axis=-1, keepdims=True)
        )
        back_sum = lax.psum(back_part.astype(jnp.bfloat16), "cores").astype(jnp.float32)
        grad_in = (upstream.astype(jnp.float32) + back_sum).astype(jnp.bfloat16)
        back_out.append(lax.dynamic_slice_in_dim(grad_in, row_start, share, 0))
        gated_list.append(gated_back.reshape(length, slab_rows))
        upstream_list.append(upstream)
        if tick_no + 1 < ticks:
            returned = from_behind(grad_in, "section", -1)
    stacked_gated = jnp.concatenate(gated_list, axis=0)
    stacked_upstream = jnp.concatenate(upstream_list, axis=0)
    product = lax.dot_general(
        stacked_gated,
        stacked_upstream,
        (((0,), (0,)), ((), ())),
        preferred_element_type=jnp.float32,
    )
    scaling = (ticks * length * lax.axis_size("dp")) ** (-0.5)
    grads_sum = (
        lax.psum_scatter(
            product.astype(jnp.bfloat16), "dp", scatter_dimension=1, tiled=True
        ).astype(jnp.float32)
        * scaling
    )
    return (jnp.stack(ahead_out)[None], jnp.stack(back_out)[None], grads_sum[None])


def solution(mesh):
    in_specs = (
        P(None, "dp", None),
        P("section", "dp", None),
        P(None, "dp", None),
        P("section", "dp", None),
        P("section", None, "dp", None),
        P("section", "dp", "cores"),
        P("section", "cores", "dp"),
        P("dp", None),
        P("dp", None),
        P("dp", None, None, None),
        P("dp", None, None, None),
    )
    out_specs = (
        P("section", None, ("dp", "cores"), None),
        P("section", None, ("dp", "cores"), None),
        P("section", "cores", "dp"),
    )
    return jax.shard_map(
        per_device, mesh=mesh, in_specs=in_specs, out_specs=out_specs, check_vma=False
    )
```

profile of v0, /device:TPU:16, one launch (start us, length us, event | category | flops | bytes accessed | tf_op | source)
XLA Modules:
  0.0 493.2 jit_solution(5450123814144851031)
XLA Ops:
  8.7 1.4 fusion.137
  13.4 1.2 fusion.72
  14.6 1.4 fusion.78
  16.0 1.0 fusion.38
  17.1 1.0 fusion.48
  18.4 73.1 %all-gather.7.cloned.1.call-done = bf16[1,512,2048]{2,1,0:T(8,128)(2,1)} async-done(((bf16[1,512,128]{2,1,0:T(8,128)(2,1)}), bf16[1,512,2048]{2,1,0:T(8,128)(2,1)}) %all-gather.7.cloned.1.call-update) | async-done | bytes 2097168 | tf_op jit(solution)/shard_map/all_gather | solution.py:132
  91.5 2.4 fusion.31
  94.6 104.7 %all-gather.5.cloned.1.call-done = bf16[1,2048,2048]{2,1,0:T(8,128)(2,1)} async-done(((bf16[1,128,2048]{2,1,0:T(8,128)(2,1)}), bf16[1,2048,2048]{2,1,0:T(8,128)(2,1)}) %all-gather.5.cloned.1.call-update) | async-done | bytes 8388624 | tf_op jit(solution)/shard_map/all_gather | solution.py:137
  199.3 5.2 %fusion.6 = f32[192,2048]{1,0:T(8,128)S(1)} fusion(bf16[1,2048,2048]{2,1,0:T(8,128)(2,1)} %all-gather.5.cloned.1.call-done, bf16[96,2048]{1,0:T(8,128)(2,1)S(1)} %get-tuple-element.54, bf16[96,2048]{1,0:T(8,128)(2,1)S(1)} %get-tuple-element.55), kind=kOutput, calls=%fused_computation.6 | convolution fusion | flops 1612185600 | bytes 10747904 | tf_op jit(solution)/shard_map/dot_general | solution.py:167
  204.7 1.0 copy-done.9
  213.4 1.4 pad_maximum_fusion
  215.3 1.2 stack.60
  216.5 6.5 %fusion.68 = (f32[96]{0:T(128)S(1)}, f32[96]{0:T(128)S(1)}, f32[96,2048]{1,0:T(8,128)S(1)}) fusion(f32[96]{0:T(128)S(1)} %add_rsqrt_fusion.6, bf16[1,2,96,2048]{3,2,1,0:T(8,128)(2,1)S(1)} %copy-done.1, bf16[1,2048,2048]{2,1,0:T(8,128)(2,1)} %all-gather.5.cloned.1.call-done, f32[96,2048]{1,0:T(8,128)} %stack.60, f32[192,2048]{1,0:T(8,128)S(1)} %copy-done.10), kind=kOutput, calls=%fused_computation.86 | convolution fusion | flops 808451840 | bytes 11535616 | tf_op jit(solution)/shard_map/sf,df->sd/dot_general | solution.py:186
  223.1 1.1 fusion.64
  224.9 1.2 convolution_convert_fusion.2
  228.5 30.0 %all-reduce.7.cloned.1.call-done = (bf16[96,2048]{1,0:T(8,128)(2,1)}, bf16[96,2048]{1,0:T(8,128)(2,1)}) async-done(((bf16[96,2048]{1,0:T(8,128)(2,1)}, bf16[96,2048]{1,0:T(8,128)(2,1)}), (bf16[96,2048]{1,0:T(8,128)(2,1)}, bf16[96,2048]{1,0:T(8,128)(2,1)})) %all-reduce.7.cloned.1.call-update) | async-done | bytes 786448 | tf_op jit(solution)/shard_map/psum | solution.py:174
  258.5 1.2 fusion.80
  259.7 8.1 %collective-permute-start = (bf16[96,2048]{1,0:T(8,128)(2,1)S(1)}, bf16[96,2048]{1,0:T(8,128)(2,1)S(1)}, u32[]{:S(2)}, u32[]{:S(2)}) collective-permute-start(bf16[96,2048]{1,0:T(8,128)(2,1)S(1)} %fusion.80), channel_id=1, source_target_pairs={{0,32},{32,64},{64,96},{96,128},{128,160},{160,192},{192,224},{224... | collective-permute-start | bytes 1179656 | tf_op jit(solution)/shard_map/ppermute | solution.py:17
  267.8 1.9 add_convert_fusion
  269.7 2.8 collective-permute-start.1
  272.5 26.8 %collective-permute-done = bf16[96,2048]{1,0:T(8,128)(2,1)S(1)} collective-permute-done((bf16[96,2048]{1,0:T(8,128)(2,1)S(1)}, bf16[96,2048]{1,0:T(8,128)(2,1)S(1)}, u32[]{:S(2)}, u32[]{:S(2)}) %collective-permute-start) | collective-permute-done | bytes 393248 | tf_op jit(solution)/shard_map/ppermute | solution.py:17
  299.7 5.2 %fusion.4 = f32[192,2048]{1,0:T(8,128)S(1)} fusion(bf16[1,2048,2048]{2,1,0:T(8,128)(2,1)} %all-gather.5.cloned.1.call-done, bf16[96,2048]{1,0:T(8,128)(2,1)S(1)} %copy-done.21, bf16[96,2048]{1,0:T(8,128)(2,1)S(1)} %multiply_convert_fusion.2), kind=kOutput, calls=%fused_computation.4 | convolution fusion | flops 1612185600 | bytes 10747904 | tf_op jit(solution)/shard_map/dot_general | solution.py:167
  304.9 1.2 copy-done.8
  306.1 1.2 fusion.157
  307.4 2.5 reshape.826
  309.9 2.4 fusion.152
  313.4 1.0 bitcast_select_fusion
  315.2 1.5 fusion.28
  316.7 1.0 reshape.834
  317.7 1.9 multiply_convert_fusion.5
  319.6 1.2 fusion.106
  320.8 1.2 fusion.21
  324.7 2.6 reshape.822
  327.3 2.5 fusion.153
  329.8 2.0 multiply_reduce_fusion.5
  331.8 1.1 fusion.97
  333.6 1.2 pad_maximum_fusion.1
  334.8 1.4 copy.67
  336.2 2.4 stack.67
  338.6 6.8 %fusion.73 = (f32[96]{0:T(128)S(1)}, f32[96,2048]{1,0:T(8,128)S(1)}) fusion(f32[96]{0:T(128)S(1)} %add_rsqrt_fusion.4, bf16[1,2,96,2048]{3,2,1,0:T(8,128)(2,1)} %param.15, bf16[1,2048,2048]{2,1,0:T(8,128)(2,1)} %all-gather.5.cloned.1.call-done, f32[96,2048]{1,0:T(8,128)} %stack.67, f32[192,2048]{1,0:T(8,128)} %copy-done.8), kind=kOutput, calls=%fused_computation.91 | convolution fusion | flops 807862144 | bytes 11141888 | tf_op jit(solution)/shard_map/sf,df->sd/dot_general | solution.py:186
  345.4 1.0 fusion.76
  346.4 1.2 convolution_convert_fusion.1
  347.9 1.7 convolution_convert_fusion
  349.6 2.5 copy.74
  354.1 35.7 %all-reduce.5.cloned.1.call-done = (bf16[96,2048]{1,0:T(8,128)(2,1)}, bf16[96,2048]{1,0:T(8,128)(2,1)}) async-done(((bf16[96,2048]{1,0:T(8,128)(2,1)}, bf16[96,2048]{1,0:T(8,128)(2,1)}), (bf16[96,2048]{1,0:T(8,128)(2,1)}, bf16[96,2048]{1,0:T(8,128)(2,1)})) %all-reduce.5.cloned.1.call-update) | async-done | bytes 786448 | tf_op jit(solution)/shard_map/psum | solution.py:174
  390.8 1.0 fusion.94
  393.3 91.6 %reduce-scatter.4.cloned.1.call-done = bf16[128,512]{1,0:T(8,128)(2,1)} async-done(((bf16[2048,512]{1,0:T(8,128)(2,1)}), bf16[128,512]{1,0:T(8,128)(2,1)}) %reduce-scatter.4.cloned.1.call-update) | async-done | bytes 131088
  484.9 1.0 copy.75
  (132 shorter events, 25.3 us)
Async XLA Ops:
  7.2 11.0 %copy-start.1 = (bf16[1,2,96,2048]{3,2,1,0:T(8,128)(2,1)S(1)}, bf16[1,2,96,2048]{3,2,1,0:T(8,128)(2,1)}, u32[]{:S(2)}) copy-start(bf16[1,2,96,2048]{3,2,1,0:T(8,128)(2,1)} %param.15) | copy-start | bytes 2359300
  7.2 10.9 %copy-start.24 = (bf16[1,96,2048]{2,1,0:T(8,128)(2,1)S(1)}, bf16[1,96,2048]{2,1,0:T(8,128)(2,1)}, u32[]{:S(2)}) copy-start(bf16[1,96,2048]{2,1,0:T(8,128)(2,1)} %param.14) | copy-start | bytes 1179652
  7.2 10.9 %copy-start.17 = (bf16[2,96,2048]{2,1,0:T(8,128)(2,1)S(1)}, bf16[2,96,2048]{2,1,0:T(8,128)(2,1)}, u32[]{:S(2)}) copy-start(bf16[2,96,2048]{2,1,0:T(8,128)(2,1)} %param.13) | copy-start | bytes 2359300
  7.2 84.3 %all-gather.7.cloned.1.call-start = ((), (), s32[]{:S(2)}) async-start(), calls=%async_computation.2 | async-start | bytes 2228224 | tf_op jit(solution)/shard_map/all_gather | solution.py:132
  7.9 191.4 %all-gather.5.cloned.1.call-start = ((), (), s32[]{:S(2)}) async-start(), calls=%async_computation.1 | async-start | bytes 8912896 | tf_op jit(solution)/shard_map/all_gather | solution.py:137
  8.7 249.8 %all-reduce.7.cloned.1.call-start = ((), (), s32[]{:S(2)}) async-start(), calls=%async_computation.5 | async-start | bytes 1572864 | tf_op jit(solution)/shard_map/psum | solution.py:174
  16.0 77.9 %copy-start.5 = (bf16[1,96,2048]{2,1,0:T(8,128)(2,1)}, bf16[1,96,2048]{2,1,0:T(8,128)(2,1)S(1)}, u32[]{:S(2)}) copy-start(bf16[1,96,2048]{2,1,0:T(8,128)(2,1)S(1)} %get-tuple-element.28) | copy-start | bytes 1179652
  204.5 1.1 copy-start.9
  206.2 0.8 copy-start.30
  206.2 1.1 copy-start.7
  210.3 1.8 copy-start.29
  213.4 3.1 copy-start.10
  223.1 1.9 copy-start
  223.1 1.9 copy-start.19
  224.2 34.3 %copy-start.6 = (bf16[1,96,2048]{2,1,0:T(8,128)(2,1)S(1)}, bf16[1,96,2048]{2,1,0:T(8,128)(2,1)}, u32[]{:S(2)}) copy-start(bf16[1,96,2048]{2,1,0:T(8,128)(2,1)} %copy-done.5) | copy-start | bytes 1179652
  226.2 163.6 %all-reduce.5.cloned.1.call-start = ((), (), s32[]{:S(2)}) async-start(), calls=%async_computation.4 | async-start | bytes 1572864 | tf_op jit(solution)/shard_map/psum | solution.py:174
  228.5 84.0 %copy-start.27 = (f32[96,96]{1,0:T(8,128)}, f32[96,96]{1,0:T(8,128)S(1)}, u32[]{:S(2)}) copy-start(f32[96,96]{1,0:T(8,128)S(1)} %fusion.53) | copy-start | bytes 110596
  258.5 40.8 %copy-start.16 = (bf16[2,96,2048]{2,1,0:T(8,128)(2,1)S(1)}, bf16[2,96,2048]{2,1,0:T(8,128)(2,1)}, u32[]{:S(2)}) copy-start(bf16[2,96,2048]{2,1,0:T(8,128)(2,1)} %param.11) | copy-start | bytes 2359300
  259.7 12.8 %copy-start.13 = (bf16[96,2048]{1,0:T(8,128)(2,1)}, bf16[96,2048]{1,0:T(8,128)(2,1)S(1)}, u32[]{:S(2)}) copy-start(bf16[96,2048]{1,0:T(8,128)(2,1)S(1)} %fusion.80) | copy-start | bytes 1179652
  259.7 40.0 %copy-start.21 = (bf16[96,2048]{1,0:T(8,128)(2,1)S(1)}, bf16[96,2048]{1,0:T(8,128)(2,1)}, u32[]{:S(2)}) copy-start(bf16[96,2048]{1,0:T(8,128)(2,1)} %get-tuple-element.37) | copy-start | bytes 1179652
  259.7 39.6 %collective-permute-start = (bf16[96,2048]{1,0:T(8,128)(2,1)S(1)}, bf16[96,2048]{1,0:T(8,128)(2,1)S(1)}, u32[]{:S(2)}, u32[]{:S(2)}) collective-permute-start(bf16[96,2048]{1,0:T(8,128)(2,1)S(1)} %fusion.80), channel_id=1, source_target_pairs={{0,32},{32,64},{64,96},{96,128},{128,160},{160,192},{192,224},{224... | collective-permute-start | bytes 1179656 | tf_op jit(solution)/shard_map/ppermute | solution.py:17
  269.7 43.7 %collective-permute-start.1 = (bf16[96,2048]{1,0:T(8,128)(2,1)}, bf16[96,2048]{1,0:T(8,128)(2,1)}, u32[]{:S(2)}, u32[]{:S(2)}) collective-permute-start(bf16[96,2048]{1,0:T(8,128)(2,1)} %add_convert_fusion), channel_id=1, source_target_pairs={{32,0},{64,32},{96,64},{128,96},{160,128},{192,160},{224,192},{256... | collective-permute-start | bytes 1179656 | tf_op jit(solution)/shard_map/ppermute | solution.py:17
  304.9 1.2 copy-start.8
  309.9 3.5 copy-start.18
  312.3 1.1 copy-start.11
  312.5 0.9 copy-start.25
  314.5 0.7 copy-start.3
  317.7 4.4 copy-start.12
  317.7 6.1 %copy-start.26 = (f32[4,96,96]{2,1,0:T(8,128)S(1)}, f32[4,96,96]{2,1,0:T(8,128)}, u32[]{:S(2)}) copy-start(f32[4,96,96]{2,1,0:T(8,128)} %copy-done.25) | copy-start | bytes 442372
  317.7 6.1 %copy-start.28 = (f32[96,96]{1,0:T(8,128)S(1)}, f32[96,96]{1,0:T(8,128)}, u32[]{:S(2)}) copy-start(f32[96,96]{1,0:T(8,128)} %copy-done.27) | copy-start | bytes 110596
  327.3 6.3 %copy-start.15 = (f32[1,96,4,1,128]{4,1,2,3,0:T(8,128)S(1)}, f32[1,96,4,1,128]{4,1,2,3,0:T(8,128)}, u32[]{:S(2)}) copy-start(f32[1,96,4,1,128]{4,1,2,3,0:T(8,128)} %get-tuple-element.39) | copy-start | bytes 589828
  338.6 6.8 %copy-start.2 = (bf16[1,2,96,2048]{3,2,1,0:T(8,128)(2,1)S(1)}, bf16[1,2,96,2048]{3,2,1,0:T(8,128)(2,1)}, u32[]{:S(2)}) copy-start(bf16[1,2,96,2048]{3,2,1,0:T(8,128)(2,1)} %param.15) | copy-start | bytes 2359300
  338.6 7.8 %copy-start.20 = (bf16[1,96,4,128]{3,2,1,0:T(4,128)(2,1)S(1)}, bf16[1,96,4,128]{3,2,1,0:T(4,128)(2,1)}, u32[]{:S(2)}) copy-start(bf16[1,96,4,128]{3,2,1,0:T(4,128)(2,1)} %copy.53) | copy-start | bytes 294916
  345.4 2.3 copy-start.22
  346.4 1.4 copy-start.23
  347.6 137.3 %reduce-scatter.4.cloned.1.call-start = ((), (), s32[]{:S(2)}) async-start(), calls=%async_computation.3 | async-start | bytes 2228224
  352.1 1.0 copy-start.14
  352.1 38.6 %copy-start.4 = (bf16[96,2048]{1,0:T(8,128)(2,1)S(1)}, bf16[96,2048]{1,0:T(8,128)(2,1)}, u32[]{:S(2)}) copy-start(bf16[96,2048]{1,0:T(8,128)(2,1)} %copy-done.3) | copy-start | bytes 1179652
Sparse Core Ops, SparseCore 0:
  10.0 81.3 all-gather.6
  93.6 105.7 all-gather.4
  226.3 32.1 all-reduce.6
  347.7 42.0 all-reduce.4
  392.5 92.4 reduce-scatter.3
where the time goes:
time: 494 us; the launch traced here: 493 us
  waiting for transfers between devices  363 us (73%)
  matrix products  45.3 us (9%)
  other arithmetic  30.4 us (6%)
  local copies, waits for them, and re-layouts  25.8 us (5%)
  between operations  17.2 us (3%)
  starting transfers between devices  11.1 us (2%)
    all_gather x1, waiting for transfers between devices, per_device(): in_full = lax.all_gather(in_weight[0], 'dp', axis=0, tiled=True)  105 us
    unnamed x6, waiting for transfers between devices  93 us
    all_gather x1, waiting for transfers between devices, per_device(): out_full = lax.all_gather(out_weight[0], 'dp', axis=1, tiled=True)  73.1 us
    psum x2, waiting for transfers between devices, per_device(): lax.psum(partial_sum.astype(jnp.bfloat16), 'cores').astype(jnp.float32)  65.7 us
    ppermute x2, waiting for transfers between devices, from_behind(): return lax.ppermute(x, axis, pairs)  26.8 us
    dot_general x2, matrix products, per_device(): jnp.einsum('sf,df->sd', grad_pre, in_full, preferred_element_type=jnp.flo...  13.3 us
    ppermute x2, starting transfers between devices, from_behind(): return lax.ppermute(x, axis, pairs)  10.9 us
    dot_general x2, matrix products, per_device(): pre_both = jnp.dot(both_normed, in_full, preferred_element_type=jnp.float32)  10.4 us
  transfers between devices with their start and end apart: 7, of which 6 were waited for; matrix products, arithmetic and copies ran while one was open for 7% of the time, Pallas kernels for 0%

commit v1 on v0

v1 whole, which is shorter than its diff:
```python
import jax
import jax.numpy as jnp
from jax import lax
from jax.experimental import pallas as pl
from jax.experimental.pallas import tpu as pltpu
from jax.sharding import PartitionSpec as P

HEAD = 128
HEADS = 4
WIDE = 4 * HEAD
BLOCK = 24
BLOCKS = 4
ROWS = BLOCK * BLOCKS
HALF = ROWS // 2
D = 2048
TICKS = 2
NZ, NX = 4, 4
NDP = NZ * NX
SHARD = D // NDP
EPSILON = 1e-06
SCALE = HEAD**-0.5
MESH = pl.DeviceIdType.MESH
F32, BF16 = jnp.float32, jnp.bfloat16

NT = (((1,), (1,)), ((), ()))
TN = (((0,), (0,)), ((), ()))


def sigmoid(v):
    return 1.0 / (1.0 + jnp.exp(-v))


def dot(a, b, dims=(((1,), (0,)), ((), ()))):
    return lax.dot_general(a, b, dims, preferred_element_type=F32)


def inverse_rms(v):
    return lax.rsqrt(jnp.mean(v * v, axis=-1, keepdims=True) + EPSILON)


def keep_count(blocks, marks, history):
    i = lax.broadcasted_iota(jnp.int32, (ROWS, ROWS), 0)
    j = lax.broadcasted_iota(jnp.int32, (ROWS, ROWS), 1)

    def owner(p):
        return sum((p >= BLOCK * b).astype(jnp.int32) for b in range(1, BLOCKS))

    bi, bj = owner(i), owner(j)
    spread = (bi == bj).astype(jnp.int32)
    for a in range(1, BLOCKS):
        for b in range(a):
            here = ((bi == a) & (bj == b)).astype(jnp.int32)
            spread = spread + here * marks[0, history, a, b]
    live = jnp.full((ROWS, ROWS), blocks[0, history] * BLOCK, jnp.int32)
    keep = (spread > 0) & (j <= i) & (i < live) & (j < live)
    return jnp.where(keep, 1.0 / live.astype(F32), 0.0)


def kernel(
    sections,
    arrivals,
    in_flight,
    cotangent,
    grad_flight,
    stashed,
    in_weight,
    out_weight,
    f_blocks,
    b_blocks,
    f_marks,
    b_marks,
    acts_out,
    grads_out,
    wgrad_out,
    win,
    wout,
    gat,
    gcol,
    xin,
    gin,
    xsrc,
    gsrc,
    stash,
    xn,
    u_s,
    part,
    dxn,
    dgat,
    dsil_s,
    gate_s,
    norm_s,
    rs_s,
    v_s,
    q_s,
    k_s,
    p_s,
    dsc_s,
    keep_s,
    esend,
    erecv,
    outs,
    wg_s,
    load_sem,
    ag_recv,
    ag_send,
    ex_send,
    ex_recv,
    sec_send,
    sec_recv,
    fw_send,
    fw_recv,
    a2a_send,
    a2a_recv,
    st_sem,
):
    s = lax.axis_index("section")
    me = lax.axis_index("dp")
    c = lax.axis_index("cores")
    z, x = me // NX, me % NX
    right, left, across = (x + 1) % NX, (x + NX - 1) % NX, (x + 2) % NX
    peer_z = (z + 1 - 2 * (z % 2), (z + 2) % NZ, NZ - 1 - z)
    zs = (z,) + peer_z
    ahead, behind = (s + 1) % sections, (s + sections - 1) % sections
    mine, other = pl.multiple_of(c * HALF, 16), pl.multiple_of((1 - c) * HALF, 16)

    barrier = pltpu.get_barrier_semaphore()
    for k in range(1, NDP):
        pl.semaphore_signal(barrier, inc=1, device_id=(s, (me + k) % NDP, c), device_id_type=MESH)
    pl.semaphore_signal(barrier, inc=1, device_id=(s, me, 1 - c), device_id_type=MESH)
    pl.semaphore_signal(barrier, inc=1, device_id=(ahead, me, c), device_id_type=MESH)
    pl.semaphore_signal(barrier, inc=1, device_id=(behind, me, c), device_id_type=MESH)

    def chunk(n, owner):
        if n == 2:
            return wout.at[:, pl.ds(pl.multiple_of(owner * SHARD, SHARD), SHARD)]
        if n == 5:
            return gat.at[:, owner]
        h = n if n < 2 else n - 1
        return win.at[h, pl.ds(pl.multiple_of(owner * SHARD, SHARD), SHARD), :]

    loads = []
    for h in range(HEADS):
        n = h if h < 2 else h + 1
        loads.append((in_weight.at[0, :, pl.ds(h * WIDE, WIDE)], chunk(n, me)))
    loads.append((out_weight.at[0], chunk(2, me)))
    loads += [
        (stashed.at[0], stash),
        (arrivals, xsrc),
        (in_flight.at[0], xin.at[0]),
        (cotangent, gsrc),
        (grad_flight.at[0], gin.at[0]),
    ]
    loads = [pltpu.make_async_copy(a, b, load_sem.at[i]) for i, (a, b) in enumerate(loads)]
    for copy in loads:
        copy.start()

    def remote(src, dst, send, recv, to):
        return pltpu.make_async_remote_copy(
            src_ref=src, dst_ref=dst, send_sem=send, recv_sem=recv, device_id=to, device_id_type=MESH
        )

    sent = []

    def ag(n, owner, slot, to_z, to_x):
        part_ref = chunk(n, owner)
        return remote(
            part_ref, part_ref, ag_send.at[n, slot], ag_recv.at[n, owner], (s, to_z * NX + to_x, c)
        )

    def push(n, owner, slot, to_z, to_x):
        copy = ag(n, owner, slot, to_z, to_x)
        copy.start()
        sent.append(copy)

    def arrive(n, owner):
        ag(n, owner, 0, z, right).wait_recv()

    def begin(n):
        push(n, me, 0, z, right)
        push(n, me, 1, z, left)
        for i in range(3):
            push(n, me, 2 + i, peer_z[i], x)

    def spread(n):
        for i in range(3):
            owner = peer_z[i] * NX + x
            arrive(n, owner)
            push(n, owner, 5 + 2 * i, z, right)
            push(n, owner, 6 + 2 * i, z, left)

    def forward(n):
        for i in range(4):
            from_left, from_right = zs[i] * NX + left, zs[i] * NX + right
            if i in (0, 3):
                arrive(n, from_left)
                push(n, from_left, 11 + i, z, right)
                arrive(n, from_right)
            else:
                arrive(n, from_right)
                push(n, from_right, 11 + i, z, left)
                arrive(n, from_left)

    def finish(n):
        for i in range(4):
            arrive(n, zs[i] * NX + across)

    loads[0].wait()
    pl.semaphore_wait(barrier, NDP - 1 + 3)
    begin(0)
    loads[1].wait()
    begin(1)

    for t in range(TICKS):
        keep_s[t] = keep_count(f_blocks, f_marks, t - s + sections - 1)
        keep_s[2 + t] = keep_count(b_blocks, b_marks, t + s)

    def normed(v):
        v = v.astype(F32)
        return (v * inverse_rms(v)).astype(BF16)

    spread(0)
    for copy in loads[2:]:
        copy.wait()
    begin(2)

    xsrc[0] = jnp.where(s == 0, xsrc[0], xin[0])
    gsrc[0] = jnp.where(s == sections - 1, gsrc[0], gin[0])
    xn[0:ROWS] = normed(xsrc[0])
    for t in range(TICKS):
        xn[ROWS * (t + 1) : ROWS * (t + 2)] = normed(stash[t])

    a2a_sent = []

    def a2a(t, k):
        to = (me + k) % NDP
        return remote(
            gsrc.at[t, :, pl.ds(pl.multiple_of(to * SHARD, SHARD), SHARD)],
            gcol.at[t, me],
            a2a_send.at[t, k],
            a2a_recv.at[t, me],
            (s, to, c),
        )

    def a2a_start(t):
        for k in range(1, NDP):
            copy = a2a(t, k)
            copy.start()
            a2a_sent.append(copy)
        gcol[t, me] = gsrc[t, :, pl.ds(pl.multiple_of(me * SHARD, SHARD), SHARD)]

    def a2a_wait(t):
        for k in range(1, NDP):
            sender = (me + k) % NDP
            remote(
                gsrc.at[t, :, pl.ds(0, SHARD)],
                gcol.at[t, sender],
                a2a_send.at[t, k],
                a2a_recv.at[t, sender],
                (s, sender, c),
            ).wait_recv()

    def heads_forward(u, keep):
        sg = sigmoid(u)
        act = u * sg
        gate = act[:, :HEAD]
        v = act[:, HEAD : 2 * HEAD].astype(BF16)
        q = act[:, 2 * HEAD : 3 * HEAD].astype(BF16)
        k = act[:, 3 * HEAD :].astype(BF16)
        scores = dot(q, k, NT) * SCALE
        ss = sigmoid(scores)
        probs = (scores * ss * keep).astype(BF16)
        mixed = dot(probs, v)
        rs = inverse_rms(mixed)
        norm = mixed * rs
        return (norm * gate).astype(BF16), (sg, gate, v, q, k, scores, ss, probs, rs, norm)

    def ahead_part(t, h, u):
        gated, _ = heads_forward(u, keep_s[t])
        more = dot(gated, wout[h * HEAD : (h + 1) * HEAD, :])
        if h == 0:
            part[...] = more
        else:
            part[...] += more

    def back_first(t, h, u):
        keep = keep_s[2 + t]
        gated, (sg, gate, v, q, k, scores, ss, probs, rs, norm) = heads_forward(u, keep)
        gat[t, me, :, h * HEAD : (h + 1) * HEAD] = gated
        dsil_s[t, h] = sg * (1.0 + u * (1.0 - sg))
        gate_s[t, h] = gate
        norm_s[t, h] = norm
        rs_s[t, h] = jnp.broadcast_to(rs, (ROWS, HEAD))
        v_s[t, h] = v
        q_s[t, h] = q
        k_s[t, h] = k
        p_s[t, h] = probs
        dsc_s[t, h] = keep * ss * (1.0 + scores * (1.0 - ss)) * SCALE

    def back_second(t, h):
        dg = dgat[:, h * HEAD : (h + 1) * HEAD].astype(F32)
        norm = norm_s[t, h]
        dn = dg * gate_s[t, h]
        dgate = dg * norm
        dm = (rs_s[t, h] * (dn - norm * jnp.mean(dn * norm, axis=-1, keepdims=True))).astype(BF16)
        dp = dot(dm, v_s[t, h], NT)
        dv = dot(p_s[t, h], dm, TN)
        ds = (dp * dsc_s[t, h]).astype(BF16)
        dq = dot(ds, k_s[t, h])
        dk = dot(ds, q_s[t, h], TN)
        du = (jnp.concatenate([dgate, dv, dq, dk], axis=1) * dsil_s[t, h]).astype(BF16)
        more = dot(du, win[h], NT)
        if h == 0:
            dxn[...] = more
        else:
            dxn[...] += more

    def gated_grad(t):
        dgat[...] = dot(gsrc[t], wout[...], NT).astype(BF16)

    def project(h):
        u_s[...] = dot(xn[...], win[h])

    def u_of(i):
        return u_s[ROWS * i : ROWS * (i + 1)]

    def exchange(i, total):
        esend[i] = total[pl.ds(other, HALF)].astype(BF16)
        copy = remote(esend.at[i], erecv.at[i], ex_send.at[i], ex_recv.at[i], (s, me, 1 - c))
        copy.start()
        sent.append(copy)
        return copy

    def ahead_end(t, copy):
        copy.wait_recv()
        out = (
            xsrc[t, pl.ds(mine, HALF)].astype(F32)
            + part[pl.ds(mine, HALF)]
            + erecv[t].astype(F32)
        )
        outs[0, t] = out.astype(BF16)

    def back_end(t, copy):
        copy.wait_recv()
        d = dxn[pl.ds(mine, HALF)] + erecv[2 + t].astype(F32)
        saved = stash[t, pl.ds(mine, HALF)].astype(F32)
        root = inverse_rms(saved)
        saved = saved * root
        back = root * (d - saved * jnp.mean(d * saved, axis=-1, keepdims=True))
        outs[1, t] = (gsrc[t, pl.ds(mine, HALF)].astype(F32) + back).astype(BF16)

    stores = []

    def store(i, t, ref):
        copy = pltpu.make_async_copy(outs.at[i, t], ref.at[0, t], st_sem.at[2 * i + t])
        copy.start()
        stores.append(copy)

    def relay(i, held, to):
        half = held.at[1, pl.ds(mine, HALF)]
        far = remote(outs.at[i, 0], half, sec_send.at[i], sec_recv.at[i], (to, me, c))
        far.start()
        sent.append(far)
        return far

    def hand_on(i, held, far):
        half = held.at[1, pl.ds(mine, HALF)]
        far.wait_recv()
        near = remote(half, half, fw_send.at[i], fw_recv.at[i], (s, me, 1 - c))
        near.start()
        sent.append(near)
        return near

    forward(0)
    spread(1)
    finish(0)
    project(0)
    ahead_later = []
    back_first(0, 0, u_of(1))
    back_first(1, 0, u_of(2))
    a_u0 = u_of(0)
    ahead_later.append(heads_forward(a_u0, keep_s[0])[0])

    forward(1)
    spread(2)
    begin(3)
    finish(1)
    project(1)
    back_first(0, 1, u_of(1))
    back_first(1, 1, u_of(2))
    ahead_later.append(heads_forward(u_of(0), keep_s[0])[0])

    forward(2)
    spread(3)
    begin(4)
    finish(2)
    part[...] = dot(jnp.concatenate(ahead_later, axis=1), wout[: 2 * HEAD, :])
    gated_grad(0)
    back_second(0, 0)
    back_second(0, 1)

    forward(3)
    spread(4)
    finish(3)
    project(2)
    ahead_part(0, 2, u_of(0))
    back_first(0, 2, u_of(1))
    back_first(1, 2, u_of(2))
    back_second(0, 2)

    forward(4)
    finish(4)
    project(3)
    ahead_part(0, 3, u_of(0))
    ahead_copy = exchange(0, part)
    back_first(0, 3, u_of(1))
    back_second(0, 3)
    back_copy = exchange(2, dxn)
    ahead_end(0, ahead_copy)
    ahead_far = relay(0, xin, ahead)
    store(0, 0, acts_out)
    back_end(0, back_copy)
    back_far = relay(1, gin, behind)
    store(1, 0, grads_out)

    back_first(1, 3, u_of(2))
    begin(5)
    a2a_start(0)
    spread(5)

    ahead_near = hand_on(0, xin, ahead_far)
    forward(5)
    ahead_near.wait_recv()
    xsrc[1] = jnp.where(s == 0, xsrc[1], xin[1])
    xn[0:ROWS] = normed(xsrc[1])
    for h in range(HEADS):
        ahead_part(1, h, dot(xn[0:ROWS], win[h]))
    ahead_copy = exchange(1, part)

    back_near = hand_on(1, gin, back_far)
    back_near.wait_recv()
    gsrc[1] = jnp.where(s == sections - 1, gsrc[1], gin[1])
    a2a_start(1)
    ahead_end(1, ahead_copy)
    store(0, 1, acts_out)
    gated_grad(1)
    for h in range(HEADS):
        back_second(1, h)
    back_copy = exchange(3, dxn)

    finish(5)
    a2a_wait(0)

    def weight_term(t):
        return dot(
            gcol[t].reshape(NDP * ROWS, SHARD), gat[t].reshape(NDP * ROWS, HEADS * HEAD), TN
        )

    total = weight_term(0)
    back_end(1, back_copy)
    store(1, 1, grads_out)
    a2a_wait(1)
    total = (total + weight_term(1)) * (TICKS * ROWS * NDP) ** -0.5
    wg_s[...] = total.T
    last = pltpu.make_async_copy(wg_s, wgrad_out.at[0], st_sem.at[4])
    last.start()
    for copy in sent + a2a_sent:
        copy.wait_send()
    for copy in stores + [last]:
        copy.wait()


def solution(mesh):
    sections = mesh.shape["section"]
    in_specs = (
        P(None, "dp", None),
        P("section", "dp", None),
        P(None, "dp", None),
        P("section", "dp", None),
        P("section", None, "dp", None),
        P("section", "dp", "cores"),
        P("section", "cores", "dp"),
        P("dp", None),
        P("dp", None),
        P("dp", None, None, None),
        P("dp", None, None, None),
    )
    out_specs = (
        P("section", None, ("dp", "cores"), None),
        P("section", None, ("dp", "cores"), None),
        P("section", "cores", "dp"),
    )
    dma, vmem = pltpu.SemaphoreType.DMA, pltpu.VMEM
    scratch = [
        vmem((HEADS, D, WIDE), BF16),
        vmem((HEADS * HEAD, D), BF16),
        vmem((TICKS, NDP, ROWS, HEADS * HEAD), BF16),
        vmem((TICKS, NDP, ROWS, SHARD), BF16),
        vmem((TICKS, ROWS, D), BF16),
        vmem((TICKS, ROWS, D), BF16),
        vmem((TICKS, ROWS, D), BF16),
        vmem((TICKS, ROWS, D), BF16),
        vmem((TICKS, ROWS, D), BF16),
        vmem((3 * ROWS, D), BF16),
        vmem((3 * ROWS, WIDE), F32),
        vmem((ROWS, D), F32),
        vmem((ROWS, D), F32),
        vmem((ROWS, HEADS * HEAD), BF16),
        vmem((TICKS, HEADS, ROWS, WIDE), F32),
        vmem((TICKS, HEADS, ROWS, HEAD), F32),
        vmem((TICKS, HEADS, ROWS, HEAD), F32),
        vmem((TICKS, HEADS, ROWS, HEAD), F32),
        vmem((TICKS, HEADS, ROWS, HEAD), BF16),
        vmem((TICKS, HEADS, ROWS, HEAD), BF16),
        vmem((TICKS, HEADS, ROWS, HEAD), BF16),
        vmem((TICKS, HEADS, ROWS, ROWS), BF16),
        vmem((TICKS, HEADS, ROWS, ROWS), F32),
        vmem((2 * TICKS, ROWS, ROWS), F32),
        vmem((2 * TICKS, HALF, D), BF16),
        vmem((2 * TICKS, HALF, D), BF16),
        vmem((2, TICKS, HALF, D), BF16),
        vmem((HEADS * HEAD, SHARD), F32),
        dma((10,)),
        dma((6, NDP)),
        dma((6, 15)),
        dma((4,)),
        dma((4,)),
        dma((2,)),
        dma((2,)),
        dma((2,)),
        dma((2,)),
        dma((TICKS, NDP)),
        dma((TICKS, NDP)),
        dma((5,)),
    ]

    def per_device(*args):
        any_spec = pl.BlockSpec(memory_space=pl.ANY)
        smem_spec = pl.BlockSpec(memory_space=pltpu.SMEM)

        def body(*refs):
            kernel(sections, *refs)

        return pl.pallas_call(
            body,
            out_shape=(
                jax.ShapeDtypeStruct((1, TICKS, HALF, D), BF16),
                jax.ShapeDtypeStruct((1, TICKS, HALF, D), BF16),
                jax.ShapeDtypeStruct((1, HEADS * HEAD, SHARD), F32),
            ),
            in_specs=[any_spec] * 7 + [smem_spec] * 4,
            out_specs=(any_spec,) * 3,
            scratch_shapes=scratch,
            compiler_params=pltpu.CompilerParams(
                collective_id=0, has_side_effects=True, vmem_limit_bytes=58 * 2**20
            ),
            name="window",
        )(*args)

    return jax.shard_map(
        per_device, mesh=mesh, in_specs=in_specs, out_specs=out_specs, check_vma=False
    )
```

time: 494 us -> 179 us (0.36)
  the two profiles are of different devices: /device:TPU:16 before, /device:TPU:1 now
where the time goes in v1:
time: 179 us
  Pallas kernels  172 us (96%)
  local copies, waits for them, and re-layouts  5.77 us (3%)
    pallas_call x1, Pallas kernels, per_device(): pl.pallas_call(body, out_shape=(jax.ShapeDtypeStruct((1, TICKS, HALF, D),...  172 us
    unnamed x11, local copies, waits for them, and re-layouts  5.77 us

profile of v1, /device:TPU:1, one launch (start us, length us, event | category | flops | bytes accessed | tf_op | source)
XLA Modules:
  0.0 178.6 jit_solution(14489187450278390173)
XLA Ops:
  0.6 0.0 copy-start.2
  0.6 1.4 copy.14.refs_9_
  2.1 0.0 copy-done.2
  2.1 0.7 copy.15.refs_10_
  2.8 172.1 %window.1 = (bf16[1,2,48,2048]{3,2,1,0:T(8,128)(2,1)}, bf16[1,2,48,2048]{3,2,1,0:T(8,128)(2,1)}, f32[1,512,128]{2,1,0:T(8,128)}) custom-call(bf16[2,96,2048]{2,1,0:T(8,128)(2,1)} %refs_0_.1, bf16[1,96,2048]{2,1,0:T(8,128)(2,1)} %refs_1_.1, bf16[2,96,2048]{2,1,0:T(8,128)(2,1)} %refs_2_.1, bf16[1,96,2048]{2,1,0:T(8,128)(2,1)} %refs_3_.1, ...), custom_call_target="tpu_custom_call" | custom-call | tf_op jit(solution)/shard_map/window/pallas_call | solution.py:543
  174.9 0.0 copy-start
  174.9 1.8 %copy.19 = bf16[1,2,48,2048]{3,2,1,0:T(8,128)(2,1)} copy(bf16[1,2,48,2048]{3,2,1,0:T(8,128)(2,1)} %get-tuple-element.6) | data formatting | bytes 786432
  176.8 0.0 copy-done
  176.8 0.0 copy-start.1
  176.8 0.7 copy.20
  177.5 0.3 copy-done.1
  177.8 0.7 copy.21
Async XLA Ops:
  0.6 1.4 copy-start.2
  174.9 1.8 %copy-start = (bf16[1,2,48,2048]{3,2,1,0:T(8,128)(2,1)S(1)}, bf16[1,2,48,2048]{3,2,1,0:T(8,128)(2,1)}, u32[]{:S(2)}) copy-start(bf16[1,2,48,2048]{3,2,1,0:T(8,128)(2,1)} %get-tuple-element.7) | copy-start | bytes 1179652
  176.8 1.1 copy-start.1

commit v2 on v1

--- a/solution.py
+++ b/solution.py
@@ -50,7 +50,7 @@
     for a in range(1, BLOCKS):
         for b in range(a):
             here = ((bi == a) & (bj == b)).astype(jnp.int32)
-            spread = spread + here * marks[0, history, a, b]
+            spread = spread + here * marks[0, a, b, history]
     live = jnp.full((ROWS, ROWS), blocks[0, history] * BLOCK, jnp.int32)
     keep = (spread > 0) & (j <= i) & (i < live) & (j < live)
     return jnp.where(keep, 1.0 / live.astype(F32), 0.0)
@@ -100,6 +100,9 @@
     erecv,
     outs,
     wg_s,
+    wsum,
+    wsend,
+    wrecv,
     load_sem,
     ag_recv,
     ag_send,
@@ -111,6 +114,8 @@
     fw_recv,
     a2a_send,
     a2a_recv,
+    w_send,
+    w_recv,
     st_sem,
 ):
     s = lax.axis_index("section")
@@ -118,8 +123,12 @@
     c = lax.axis_index("cores")
     z, x = me // NX, me % NX
     right, left, across = (x + 1) % NX, (x + NX - 1) % NX, (x + 2) % NX
-    peer_z = (z + 1 - 2 * (z % 2), (z + 2) % NZ, NZ - 1 - z)
+    near_z = z - 1 + 2 * ((NZ - 1 - z) // (NZ - 1))
+    far_z = (NZ - 1) * (1 - z // 2)
+    peer_z = (near_z, 6 - z - near_z - far_z, far_z)
     zs = (z,) + peer_z
+    inner = z % (NZ - 1) != 0
+    hop_z = (z + 1, z - 1, (NZ - 1) * (z - 1))
     ahead, behind = (s + 1) % sections, (s + sections - 1) % sections
     mine, other = pl.multiple_of(c * HALF, 16), pl.multiple_of((1 - c) * HALF, 16)
 
@@ -131,18 +140,16 @@
     pl.semaphore_signal(barrier, inc=1, device_id=(behind, me, c), device_id_type=MESH)
 
     def chunk(n, owner):
-        if n == 2:
+        if n == HEADS:
             return wout.at[:, pl.ds(pl.multiple_of(owner * SHARD, SHARD), SHARD)]
-        if n == 5:
-            return gat.at[:, owner]
-        h = n if n < 2 else n - 1
-        return win.at[h, pl.ds(pl.multiple_of(owner * SHARD, SHARD), SHARD), :]
+        if n == HEADS + 1:
+            return gat.at[:, owner % NX]
+        return win.at[n, pl.ds(pl.multiple_of(owner * SHARD, SHARD), SHARD), :]
 
     loads = []
     for h in range(HEADS):
-        n = h if h < 2 else h + 1
-        loads.append((in_weight.at[0, :, pl.ds(h * WIDE, WIDE)], chunk(n, me)))
-    loads.append((out_weight.at[0], chunk(2, me)))
+        loads.append((in_weight.at[0, :, pl.ds(h * WIDE, WIDE)], chunk(h, me)))
+    loads.append((out_weight.at[0], chunk(HEADS, me)))
     loads += [
         (stashed.at[0], stash),
         (arrivals, xsrc),
@@ -161,16 +168,21 @@
 
     sent = []
 
+    def start(copy, cond=None):
+        if cond is None:
+            copy.start()
+        else:
+            pl.when(cond)(copy.start)
+        sent.append((copy, cond))
+
     def ag(n, owner, slot, to_z, to_x):
-        part_ref = chunk(n, owner)
+        block = chunk(n, owner)
         return remote(
-            part_ref, part_ref, ag_send.at[n, slot], ag_recv.at[n, owner], (s, to_z * NX + to_x, c)
+            block, block, ag_send.at[n, slot], ag_recv.at[n, owner], (s, to_z * NX + to_x, c)
         )
 
-    def push(n, owner, slot, to_z, to_x):
-        copy = ag(n, owner, slot, to_z, to_x)
-        copy.start()
-        sent.append(copy)
+    def push(n, owner, slot, to_z, to_x, cond=None):
+        start(ag(n, owner, slot, to_z, to_x), cond)
 
     def arrive(n, owner):
         ag(n, owner, 0, z, right).wait_recv()
@@ -178,35 +190,61 @@
     def begin(n):
         push(n, me, 0, z, right)
         push(n, me, 1, z, left)
-        for i in range(3):
-            push(n, me, 2 + i, peer_z[i], x)
+        push(n, me, 2, z + 1, x, z < NZ - 1)
+        push(n, me, 3, z - 1, x, z > 0)
 
     def spread(n):
         for i in range(3):
             owner = peer_z[i] * NX + x
             arrive(n, owner)
-            push(n, owner, 5 + 2 * i, z, right)
-            push(n, owner, 6 + 2 * i, z, left)
+            push(n, owner, 10 + i, hop_z[i], x, inner)
+            push(n, owner, 4 + 2 * i, z, right)
+            push(n, owner, 5 + 2 * i, z, left)
 
     def forward(n):
         for i in range(4):
             from_left, from_right = zs[i] * NX + left, zs[i] * NX + right
             if i in (0, 3):
                 arrive(n, from_left)
-                push(n, from_left, 11 + i, z, right)
+                push(n, from_left, 13 + i, z, right)
                 arrive(n, from_right)
             else:
                 arrive(n, from_right)
-                push(n, from_right, 11 + i, z, left)
+                push(n, from_right, 13 + i, z, left)
                 arrive(n, from_left)
 
     def finish(n):
         for i in range(4):
             arrive(n, zs[i] * NX + across)
 
+    xs = (x, right, left, across)
+    OUT, GATED = HEADS, HEADS + 1
+
+    def ring(n):
+        for i in range(1, NX):
+            push(n, me, i - 1, z, xs[i])
+
+    def line(i):
+        owner = z * NX + xs[i]
+        if i:
+            arrive(OUT, owner)
+        for k in range(3):
+            push(OUT, owner, 3 + 3 * i + k, peer_z[k], xs[0])
+
+    def finish_line():
+        for i in range(NX):
+            for k in range(3):
+                arrive(OUT, peer_z[k] * NX + xs[i])
+
+    def finish_ring():
+        for i in range(1, NX):
+            arrive(GATED, z * NX + xs[i])
+
     loads[0].wait()
     pl.semaphore_wait(barrier, NDP - 1 + 3)
     begin(0)
+    loads[HEADS].wait()
+    ring(OUT)
     loads[1].wait()
     begin(1)
 
@@ -219,9 +257,9 @@
         return (v * inverse_rms(v)).astype(BF16)
 
     spread(0)
-    for copy in loads[2:]:
+    line(0)
+    for copy in loads[2:HEADS] + loads[HEADS + 1 :]:
         copy.wait()
-    begin(2)
 
     xsrc[0] = jnp.where(s == 0, xsrc[0], xin[0])
     gsrc[0] = jnp.where(s == sections - 1, gsrc[0], gin[0])
@@ -229,35 +267,28 @@
     for t in range(TICKS):
         xn[ROWS * (t + 1) : ROWS * (t + 2)] = normed(stash[t])
 
-    a2a_sent = []
-
-    def a2a(t, k):
-        to = (me + k) % NDP
+    def columns(owner_z, owner_x):
+        return pl.ds(pl.multiple_of((owner_z * NX + owner_x) * SHARD, SHARD), SHARD)
+
+    def a2a(t, i, owner_z, sender):
         return remote(
-            gsrc.at[t, :, pl.ds(pl.multiple_of(to * SHARD, SHARD), SHARD)],
-            gcol.at[t, me],
-            a2a_send.at[t, k],
-            a2a_recv.at[t, me],
-            (s, to, c),
+            gsrc.at[t, :, columns(owner_z, xs[i])],
+            gcol.at[t, sender, :, pl.ds(owner_z * SHARD, SHARD)],
+            a2a_send.at[t, i, owner_z],
+            a2a_recv.at[t, sender, owner_z],
+            (s, z * NX + xs[i], c),
         )
 
     def a2a_start(t):
-        for k in range(1, NDP):
-            copy = a2a(t, k)
-            copy.start()
-            a2a_sent.append(copy)
-        gcol[t, me] = gsrc[t, :, pl.ds(pl.multiple_of(me * SHARD, SHARD), SHARD)]
+        for owner_z in range(NZ):
+            for i in range(1, NX):
+                start(a2a(t, i, owner_z, x))
+            gcol[t, x, :, owner_z * SHARD : (owner_z + 1) * SHARD] = gsrc[t, :, columns(owner_z, x)]
 
     def a2a_wait(t):
-        for k in range(1, NDP):
-            sender = (me + k) % NDP
-            remote(
-                gsrc.at[t, :, pl.ds(0, SHARD)],
-                gcol.at[t, sender],
-                a2a_send.at[t, k],
-                a2a_recv.at[t, sender],
-                (s, sender, c),
-            ).wait_recv()
+        for owner_z in range(NZ):
+            for i in range(1, NX):
+                a2a(t, i, owner_z, xs[i]).wait_recv()
 
     def heads_forward(u, keep):
         sg = sigmoid(u)
@@ -285,7 +316,7 @@
     def back_first(t, h, u):
         keep = keep_s[2 + t]
         gated, (sg, gate, v, q, k, scores, ss, probs, rs, norm) = heads_forward(u, keep)
-        gat[t, me, :, h * HEAD : (h + 1) * HEAD] = gated
+        gat[t, x, :, h * HEAD : (h + 1) * HEAD] = gated
         dsil_s[t, h] = sg * (1.0 + u * (1.0 - sg))
         gate_s[t, h] = gate
         norm_s[t, h] = norm
@@ -326,8 +357,7 @@
     def exchange(i, total):
         esend[i] = total[pl.ds(other, HALF)].astype(BF16)
         copy = remote(esend.at[i], erecv.at[i], ex_send.at[i], ex_recv.at[i], (s, me, 1 - c))
-        copy.start()
-        sent.append(copy)
+        start(copy)
         return copy
 
     def ahead_end(t, copy):
@@ -358,113 +388,127 @@
     def relay(i, held, to):
         half = held.at[1, pl.ds(mine, HALF)]
         far = remote(outs.at[i, 0], half, sec_send.at[i], sec_recv.at[i], (to, me, c))
-        far.start()
-        sent.append(far)
+        start(far)
         return far
 
     def hand_on(i, held, far):
         half = held.at[1, pl.ds(mine, HALF)]
         far.wait_recv()
         near = remote(half, half, fw_send.at[i], fw_recv.at[i], (s, me, 1 - c))
-        near.start()
-        sent.append(near)
+        start(near)
         return near
+
+    gated_ahead = []
+
+    def first(h):
+        project(h)
+        for t in range(TICKS):
+            back_first(t, h, u_of(1 + t))
+        gated_ahead.append(heads_forward(u_of(0), keep_s[0])[0])
 
     forward(0)
     spread(1)
+    begin(2)
+    line(1)
     finish(0)
-    project(0)
-    ahead_later = []
-    back_first(0, 0, u_of(1))
-    back_first(1, 0, u_of(2))
-    a_u0 = u_of(0)
-    ahead_later.append(heads_forward(a_u0, keep_s[0])[0])
+    first(0)
 
     forward(1)
     spread(2)
     begin(3)
+    line(2)
     finish(1)
-    project(1)
-    back_first(0, 1, u_of(1))
-    back_first(1, 1, u_of(2))
-    ahead_later.append(heads_forward(u_of(0), keep_s[0])[0])
+    first(1)
 
     forward(2)
     spread(3)
-    begin(4)
+    line(3)
     finish(2)
-    part[...] = dot(jnp.concatenate(ahead_later, axis=1), wout[: 2 * HEAD, :])
+    first(2)
+
+    forward(3)
+    finish_line()
+    part[...] = dot(jnp.concatenate(gated_ahead, axis=1), wout[: 3 * HEAD, :])
     gated_grad(0)
-    back_second(0, 0)
-    back_second(0, 1)
-
-    forward(3)
-    spread(4)
+    for h in range(3):
+        back_second(0, h)
+
     finish(3)
-    project(2)
-    ahead_part(0, 2, u_of(0))
-    back_first(0, 2, u_of(1))
-    back_first(1, 2, u_of(2))
-    back_second(0, 2)
-
-    forward(4)
-    finish(4)
     project(3)
-    ahead_part(0, 3, u_of(0))
-    ahead_copy = exchange(0, part)
     back_first(0, 3, u_of(1))
     back_second(0, 3)
     back_copy = exchange(2, dxn)
+    ahead_part(0, 3, u_of(0))
+    ahead_copy = exchange(0, part)
+    back_end(0, back_copy)
+    back_far = relay(1, gin, behind)
+    store(1, 0, grads_out)
     ahead_end(0, ahead_copy)
     ahead_far = relay(0, xin, ahead)
     store(0, 0, acts_out)
-    back_end(0, back_copy)
-    back_far = relay(1, gin, behind)
-    store(1, 0, grads_out)
 
     back_first(1, 3, u_of(2))
-    begin(5)
+    ring(GATED)
     a2a_start(0)
-    spread(5)
+    finish_ring()
+    a2a_wait(0)
+
+    def weight_term(t):
+        return dot(gat[t].reshape(NX * ROWS, HEADS * HEAD), gcol[t].reshape(NX * ROWS, NZ * SHARD), TN)
+
+    wsum[...] = weight_term(0)
+
+    back_near = hand_on(1, gin, back_far)
+    back_near.wait_recv()
+    gsrc[1] = jnp.where(s == sections - 1, gsrc[1], gin[1])
+    a2a_start(1)
+    gated_grad(1)
+    back_second(1, 0)
+    back_second(1, 1)
+
+    a2a_wait(1)
+    wsum[...] += weight_term(1)
+
+    def wblock(owner_z):
+        return wsum[:, pl.ds(pl.multiple_of(owner_z * SHARD, SHARD), SHARD)]
+
+    def wcopy(i, sender):
+        return remote(
+            wsend.at[i], wrecv.at[sender], w_send.at[i], w_recv.at[sender], (s, peer_z[i] * NX + x, c)
+        )
+
+    for i in range(3):
+        wsend[i] = wblock(peer_z[i]).astype(BF16)
+        start(wcopy(i, z))
+
+    back_second(1, 2)
+    back_second(1, 3)
+    back_copy = exchange(3, dxn)
 
     ahead_near = hand_on(0, xin, ahead_far)
-    forward(5)
     ahead_near.wait_recv()
     xsrc[1] = jnp.where(s == 0, xsrc[1], xin[1])
     xn[0:ROWS] = normed(xsrc[1])
     for h in range(HEADS):
         ahead_part(1, h, dot(xn[0:ROWS], win[h]))
     ahead_copy = exchange(1, part)
-
-    back_near = hand_on(1, gin, back_far)
-    back_near.wait_recv()
-    gsrc[1] = jnp.where(s == sections - 1, gsrc[1], gin[1])
-    a2a_start(1)
+    back_end(1, back_copy)
+    store(1, 1, grads_out)
     ahead_end(1, ahead_copy)
     store(0, 1, acts_out)
-    gated_grad(1)
-    for h in range(HEADS):
-        back_second(1, h)
-    back_copy = exchange(3, dxn)
-
-    finish(5)
-    a2a_wait(0)
-
-    def weight_term(t):
-        return dot(
-            gcol[t].reshape(NDP * ROWS, SHARD), gat[t].reshape(NDP * ROWS, HEADS * HEAD), TN
-        )
-
-    total = weight_term(0)
-    back_end(1, back_copy)
-    store(1, 1, grads_out)
-    a2a_wait(1)
-    total = (total + weight_term(1)) * (TICKS * ROWS * NDP) ** -0.5
-    wg_s[...] = total.T
+
+    total = wblock(z)
+    for i in range(3):
+        wcopy(i, peer_z[i]).wait_recv()
+        total = total + wrecv[peer_z[i]].astype(F32)
+    wg_s[...] = total * (TICKS * ROWS * NDP) ** -0.5
     last = pltpu.make_async_copy(wg_s, wgrad_out.at[0], st_sem.at[4])
     last.start()
-    for copy in sent + a2a_sent:
-        copy.wait_send()
+    for copy, cond in sent:
+        if cond is None:
+            copy.wait_send()
+        else:
+            pl.when(cond)(copy.wait_send)
     for copy in stores + [last]:
         copy.wait()
 
@@ -493,8 +537,8 @@
     scratch = [
         vmem((HEADS, D, WIDE), BF16),
         vmem((HEADS * HEAD, D), BF16),
-        vmem((TICKS, NDP, ROWS, HEADS * HEAD), BF16),
-        vmem((TICKS, NDP, ROWS, SHARD), BF16),
+        vmem((TICKS, NX, ROWS, HEADS * HEAD), BF16),
+        vmem((TICKS, NX, ROWS, NZ * SHARD), BF16),
         vmem((TICKS, ROWS, D), BF16),
         vmem((TICKS, ROWS, D), BF16),
         vmem((TICKS, ROWS, D), BF16),
@@ -519,21 +563,27 @@
         vmem((2 * TICKS, HALF, D), BF16),
         vmem((2, TICKS, HALF, D), BF16),
         vmem((HEADS * HEAD, SHARD), F32),
+        vmem((HEADS * HEAD, NZ * SHARD), F32),
+        vmem((3, HEADS * HEAD, SHARD), BF16),
+        vmem((NZ, HEADS * HEAD, SHARD), BF16),
         dma((10,)),
         dma((6, NDP)),
-        dma((6, 15)),
+        dma((6, 17)),
         dma((4,)),
         dma((4,)),
         dma((2,)),
         dma((2,)),
         dma((2,)),
         dma((2,)),
-        dma((TICKS, NDP)),
-        dma((TICKS, NDP)),
+        dma((TICKS, NX, NZ)),
+        dma((TICKS, NX, NZ)),
+        dma((3,)),
+        dma((NZ,)),
         dma((5,)),
     ]
 
     def per_device(*args):
+        marks = [jnp.transpose(m, (0, 2, 3, 1)) for m in args[9:]]
         any_spec = pl.BlockSpec(memory_space=pl.ANY)
         smem_spec = pl.BlockSpec(memory_space=pltpu.SMEM)
 
@@ -554,7 +604,7 @@
                 collective_id=0, has_side_effects=True, vmem_limit_bytes=58 * 2**20
             ),
             name="window",
-        )(*args)
+        )(*args[:9], *marks)
 
     return jax.shard_map(
         per_device, mesh=mesh, in_specs=in_specs, out_specs=out_specs, check_vma=False

time: 179 us -> 145 us (0.81)
  Pallas kernels: 172 us -> 141 us
  local copies, waits for them, and re-layouts: 5.77 us -> 3.61 us
    pallas_call x1, Pallas kernels: 172 us -> 141 us  [per_device(): pl.pallas_call(body, out_shape=(jax.ShapeDtypeStruct((1, TICKS, HALF, D),...]
    unnamed x11 -> x7, local copies, waits for them, and re-layouts: 5.77 us -> 3.61 us
where the time goes in v2:
time: 145 us
  Pallas kernels  141 us (97%)
  local copies, waits for them, and re-layouts  3.61 us (2%)
    pallas_call x1, Pallas kernels, per_device(): pl.pallas_call(body, out_shape=(jax.ShapeDtypeStruct((1, TICKS, HALF, D),...  141 us
    unnamed x7, local copies, waits for them, and re-layouts  3.61 us

profile of v2, /device:TPU:1, one launch (start us, length us, event | category | flops | bytes accessed | tf_op | source)
XLA Modules:
  0.0 144.9 jit_solution(4677199960239579683)
XLA Ops:
  0.6 140.6 %window.1 = (bf16[1,2,48,2048]{3,2,1,0:T(8,128)(2,1)}, bf16[1,2,48,2048]{3,2,1,0:T(8,128)(2,1)}, f32[1,512,128]{2,1,0:T(8,128)}) custom-call(bf16[2,96,2048]{2,1,0:T(8,128)(2,1)} %refs_0_.1, bf16[1,96,2048]{2,1,0:T(8,128)(2,1)} %refs_1_.1, bf16[2,96,2048]{2,1,0:T(8,128)(2,1)} %refs_2_.1, bf16[1,96,2048]{2,1,0:T(8,128)(2,1)} %refs_3_.1, ...), custom_call_target="tpu_custom_call" | custom-call | tf_op jit(solution)/shard_map/window/pallas_call | solution.py:593
  141.3 0.0 copy-start
  141.3 1.8 %copy.17 = bf16[1,2,48,2048]{3,2,1,0:T(8,128)(2,1)} copy(bf16[1,2,48,2048]{3,2,1,0:T(8,128)(2,1)} %get-tuple-element.6) | data formatting | bytes 786432
  143.1 0.0 copy-done
  143.1 0.0 copy-start.1
  143.1 0.7 copy.18
  143.8 0.3 copy-done.1
  144.2 0.7 copy.19
Async XLA Ops:
  141.3 1.8 %copy-start = (bf16[1,2,48,2048]{3,2,1,0:T(8,128)(2,1)S(1)}, bf16[1,2,48,2048]{3,2,1,0:T(8,128)(2,1)}, u32[]{:S(2)}) copy-start(bf16[1,2,48,2048]{3,2,1,0:T(8,128)(2,1)} %get-tuple-element.7) | copy-start | bytes 1179652
  143.1 1.1 copy-start.1

commit v3 on v2

--- a/solution.py
+++ b/solution.py
@@ -6,6 +6,7 @@
 from jax.sharding import PartitionSpec as P
 
 HEAD = 128
+AHEAD_AFTER = 2
 HEADS = 4
 WIDE = 4 * HEAD
 BLOCK = 24
@@ -16,6 +17,7 @@
 TICKS = 2
 NZ, NX = 4, 4
 NDP = NZ * NX
+PARTS = D // WIDE
 SHARD = D // NDP
 EPSILON = 1e-06
 SCALE = HEAD**-0.5
@@ -86,6 +88,8 @@
     part,
     dxn,
     dgat,
+    dgat_s,
+    u_next,
     dsil_s,
     gate_s,
     norm_s,
@@ -114,6 +118,8 @@
     fw_recv,
     a2a_send,
     a2a_recv,
+    pair_send,
+    pair_recv,
     w_send,
     w_recv,
     st_sem,
@@ -143,7 +149,9 @@
         if n == HEADS:
             return wout.at[:, pl.ds(pl.multiple_of(owner * SHARD, SHARD), SHARD)]
         if n == HEADS + 1:
-            return gat.at[:, owner % NX]
+            return gat.at[0, owner % NX]
+        if n == HEADS + 2:
+            return gat.at[1, owner % NX]
         return win.at[n, pl.ds(pl.multiple_of(owner * SHARD, SHARD), SHARD), :]
 
     loads = []
@@ -224,6 +232,16 @@
         for i in range(1, NX):
             push(n, me, i - 1, z, xs[i])
 
+    def ring_both():
+        for t in range(TICKS):
+            push(GATED + t, me, 0, z, right)
+            push(GATED + t, me, 1, z, left)
+
+    def pass_ring():
+        for t in range(TICKS):
+            arrive(GATED + t, z * NX + (left, right)[t])
+            push(GATED + t, z * NX + (left, right)[t], 2, z, (right, left)[t])
+
     def line(i):
         owner = z * NX + xs[i]
         if i:
@@ -237,8 +255,9 @@
                 arrive(OUT, peer_z[k] * NX + xs[i])
 
     def finish_ring():
-        for i in range(1, NX):
-            arrive(GATED, z * NX + xs[i])
+        for t in range(TICKS):
+            arrive(GATED + t, z * NX + (right, left)[t])
+            arrive(GATED + t, z * NX + across)
 
     loads[0].wait()
     pl.semaphore_wait(barrier, NDP - 1 + 3)
@@ -272,23 +291,33 @@
 
     def a2a(t, i, owner_z, sender):
         return remote(
-            gsrc.at[t, :, columns(owner_z, xs[i])],
-            gcol.at[t, sender, :, pl.ds(owner_z * SHARD, SHARD)],
+            gsrc.at[t, pl.ds(mine, HALF), columns(owner_z, xs[i])],
+            gcol.at[t, sender, pl.ds(mine, HALF), pl.ds(owner_z * SHARD, SHARD)],
             a2a_send.at[t, i, owner_z],
             a2a_recv.at[t, sender, owner_z],
             (s, z * NX + xs[i], c),
         )
 
-    def a2a_start(t):
-        for owner_z in range(NZ):
+    def a2a_start(t, *only):
+        for owner_z in only or range(NZ):
             for i in range(1, NX):
                 start(a2a(t, i, owner_z, x))
+
+    def pair(t, i):
+        half = gcol.at[t, xs[i], pl.ds(mine, HALF)]
+        return remote(half, half, pair_send.at[t, i], pair_recv.at[t, i], (s, me, 1 - c))
+
+    def a2a_pass(t):
+        for i in range(1, NX):
+            for owner_z in range(NZ):
+                a2a(t, i, owner_z, xs[i]).wait_recv()
+            start(pair(t, i))
+        for owner_z in range(NZ):
             gcol[t, x, :, owner_z * SHARD : (owner_z + 1) * SHARD] = gsrc[t, :, columns(owner_z, x)]
 
     def a2a_wait(t):
-        for owner_z in range(NZ):
-            for i in range(1, NX):
-                a2a(t, i, owner_z, xs[i]).wait_recv()
+        for i in range(1, NX):
+            pair(t, i).wait_recv()
 
     def heads_forward(u, keep):
         sg = sigmoid(u)
@@ -385,18 +414,34 @@
         copy.start()
         stores.append(copy)
 
+    def quarter(n):
+        return slice(n * WIDE, (n + 1) * WIDE)
+
     def relay(i, held, to):
-        half = held.at[1, pl.ds(mine, HALF)]
-        far = remote(outs.at[i, 0], half, sec_send.at[i], sec_recv.at[i], (to, me, c))
-        start(far)
-        return far
-
-    def hand_on(i, held, far):
-        half = held.at[1, pl.ds(mine, HALF)]
-        far.wait_recv()
-        near = remote(half, half, fw_send.at[i], fw_recv.at[i], (s, me, 1 - c))
+        copies = []
+        for n in range(PARTS):
+            half = held.at[1, pl.ds(mine, HALF), quarter(n)]
+            copy = remote(
+                outs.at[i, 0, :, quarter(n)], half, sec_send.at[i, n], sec_recv.at[i, n], (to, me, c)
+            )
+            start(copy)
+            copies.append(copy)
+        return copies
+
+    def hand_on(i, n, held, far):
+        half = held.at[1, pl.ds(mine, HALF), quarter(n)]
+        far[n].wait_recv()
+        near = remote(half, half, fw_send.at[i, n], fw_recv.at[i, n], (s, me, 1 - c))
         start(near)
         return near
+
+    def drain():
+        for copy, cond in sent:
+            if cond is None:
+                copy.wait_send()
+            else:
+                pl.when(cond)(copy.wait_send)
+        sent.clear()
 
     gated_ahead = []
 
@@ -433,39 +478,88 @@
     for h in range(3):
         back_second(0, h)
 
-    finish(3)
-    project(3)
+    for i in range(NZ):
+        arrive(3, zs[i] * NX + across)
+        rows = pl.ds(pl.multiple_of(zs[i] * WIDE, WIDE), WIDE)
+        more = dot(xn[:, rows], win[3, rows, :])
+        if i == 0:
+            u_s[...] = more
+        else:
+            u_s[...] += more
     back_first(0, 3, u_of(1))
     back_second(0, 3)
     back_copy = exchange(2, dxn)
     ahead_part(0, 3, u_of(0))
     ahead_copy = exchange(0, part)
+    drained = sent[:-2]
+    del sent[:-2]
     back_end(0, back_copy)
     back_far = relay(1, gin, behind)
     store(1, 0, grads_out)
     ahead_end(0, ahead_copy)
-    ahead_far = relay(0, xin, ahead)
     store(0, 0, acts_out)
 
     back_first(1, 3, u_of(2))
-    ring(GATED)
+    ring_both()
     a2a_start(0)
+    held_back = sent[:]
+    sent[:] = drained
+    drain()
+    sent[:] = held_back
+
+    def weight_term(t):
+        return dot(gat[t].reshape(NX * ROWS, HEADS * HEAD), gcol[t].reshape(NX * ROWS, NZ * SHARD), TN)
+
+    def back_quarter(n, near):
+        near.wait_recv()
+        gsrc[1, pl.ds(other, HALF), quarter(n)] = jnp.where(
+            s == sections - 1,
+            gsrc[1, pl.ds(other, HALF), quarter(n)],
+            gin[1, pl.ds(other, HALF), quarter(n)],
+        )
+        more = dot(gsrc[1, :, quarter(n)], wout[:, quarter(n)], NT)
+        if n == 0:
+            dgat_s[...] = more
+        else:
+            dgat_s[...] += more
+
+    def ahead_quarter(n, near):
+        near.wait_recv()
+        rows = jnp.where(s == 0, xsrc[1, :, quarter(n)], xin[1, :, quarter(n)])
+        xsrc[1, :, quarter(n)] = rows
+        for h in range(HEADS):
+            more = dot(rows, win[h, quarter(n), :])
+            if n == 0:
+                u_next[h] = more
+            else:
+                u_next[h] += more
+
+    nears = []
+    for n in range(PARTS):
+        nears.append(hand_on(1, n, gin, back_far))
+        gsrc[1, pl.ds(mine, HALF), quarter(n)] = jnp.where(
+            s == sections - 1,
+            gsrc[1, pl.ds(mine, HALF), quarter(n)],
+            gin[1, pl.ds(mine, HALF), quarter(n)],
+        )
+        a2a_start(1, n)
+        if n == 1:
+            pass_ring()
+        if n == 2:
+            a2a_pass(0)
+        if n == AHEAD_AFTER:
+            ahead_far = relay(0, xin, ahead)
+        if n:
+            back_quarter(n - 1, nears[n - 1])
+    back_quarter(PARTS - 1, nears[-1])
+    a2a_pass(1)
+    dgat[...] = dgat_s[...].astype(BF16)
+    back_second(1, 0)
+    back_second(1, 1)
+
     finish_ring()
     a2a_wait(0)
-
-    def weight_term(t):
-        return dot(gat[t].reshape(NX * ROWS, HEADS * HEAD), gcol[t].reshape(NX * ROWS, NZ * SHARD), TN)
-
     wsum[...] = weight_term(0)
-
-    back_near = hand_on(1, gin, back_far)
-    back_near.wait_recv()
-    gsrc[1] = jnp.where(s == sections - 1, gsrc[1], gin[1])
-    a2a_start(1)
-    gated_grad(1)
-    back_second(1, 0)
-    back_second(1, 1)
-
     a2a_wait(1)
     wsum[...] += weight_term(1)
 
@@ -481,19 +575,23 @@
         wsend[i] = wblock(peer_z[i]).astype(BF16)
         start(wcopy(i, z))
 
+    nears = [hand_on(0, 0, xin, ahead_far)]
     back_second(1, 2)
+    nears.append(hand_on(0, 1, xin, ahead_far))
     back_second(1, 3)
     back_copy = exchange(3, dxn)
-
-    ahead_near = hand_on(0, xin, ahead_far)
-    ahead_near.wait_recv()
-    xsrc[1] = jnp.where(s == 0, xsrc[1], xin[1])
-    xn[0:ROWS] = normed(xsrc[1])
-    for h in range(HEADS):
-        ahead_part(1, h, dot(xn[0:ROWS], win[h]))
-    ahead_copy = exchange(1, part)
+    ahead_quarter(0, nears[0])
+    nears.append(hand_on(0, 2, xin, ahead_far))
+    ahead_quarter(1, nears[1])
+    nears.append(hand_on(0, 3, xin, ahead_far))
+    ahead_quarter(2, nears[2])
     back_end(1, back_copy)
     store(1, 1, grads_out)
+    ahead_quarter(3, nears[3])
+    root = inverse_rms(xsrc[1].astype(F32))
+    gated = [heads_forward(u_next[h] * root, keep_s[1])[0] for h in range(HEADS)]
+    part[...] = dot(jnp.concatenate(gated, axis=1), wout[...])
+    ahead_copy = exchange(1, part)
     ahead_end(1, ahead_copy)
     store(0, 1, acts_out)
 
@@ -504,11 +602,7 @@
     wg_s[...] = total * (TICKS * ROWS * NDP) ** -0.5
     last = pltpu.make_async_copy(wg_s, wgrad_out.at[0], st_sem.at[4])
     last.start()
-    for copy, cond in sent:
-        if cond is None:
-            copy.wait_send()
-        else:
-            pl.when(cond)(copy.wait_send)
+    drain()
     for copy in stores + [last]:
         copy.wait()
 
@@ -549,6 +643,8 @@
         vmem((ROWS, D), F32),
         vmem((ROWS, D), F32),
         vmem((ROWS, HEADS * HEAD), BF16),
+        vmem((ROWS, HEADS * HEAD), F32),
+        vmem((HEADS, ROWS, WIDE), F32),
         vmem((TICKS, HEADS, ROWS, WIDE), F32),
         vmem((TICKS, HEADS, ROWS, HEAD), F32),
         vmem((TICKS, HEADS, ROWS, HEAD), F32),
@@ -567,16 +663,18 @@
         vmem((3, HEADS * HEAD, SHARD), BF16),
         vmem((NZ, HEADS * HEAD, SHARD), BF16),
         dma((10,)),
-        dma((6, NDP)),
-        dma((6, 17)),
+        dma((HEADS + 3, NDP)),
+        dma((HEADS + 3, 17)),
         dma((4,)),
         dma((4,)),
-        dma((2,)),
-        dma((2,)),
-        dma((2,)),
-        dma((2,)),
+        dma((2, PARTS)),
+        dma((2, PARTS)),
+        dma((2, PARTS)),
+        dma((2, PARTS)),
         dma((TICKS, NX, NZ)),
         dma((TICKS, NX, NZ)),
+        dma((TICKS, NX)),
+        dma((TICKS, NX)),
         dma((3,)),
         dma((NZ,)),
         dma((5,)),
@@ -590,7 +688,7 @@
         def body(*refs):
             kernel(sections, *refs)
 
-        return pl.pallas_call(
+        results = pl.pallas_call(
             body,
             out_shape=(
                 jax.ShapeDtypeStruct((1, TICKS, HALF, D), BF16),
@@ -606,6 +704,27 @@
             name="window",
         )(*args[:9], *marks)
 
+        def put(*refs):
+            held, sems = refs[6:9], refs[9]
+            loads = [pltpu.make_async_copy(refs[i], held[i], sems.at[i]) for i in range(3)]
+            stores = [pltpu.make_async_copy(held[i], refs[3 + i], sems.at[3 + i]) for i in range(3)]
+            for copy in loads:
+                copy.start()
+            for load, keep in zip(loads, stores):
+                load.wait()
+                keep.start()
+            for copy in stores:
+                copy.wait()
+
+        return pl.pallas_call(
+            put,
+            out_shape=tuple(jax.ShapeDtypeStruct(r.shape, r.dtype) for r in results),
+            in_specs=[any_spec] * 3,
+            out_specs=(any_spec,) * 3,
+            scratch_shapes=[vmem(r.shape, r.dtype) for r in results] + [dma((6,))],
+            name="put",
+        )(*results)
+
     return jax.shard_map(
         per_device, mesh=mesh, in_specs=in_specs, out_specs=out_specs, check_vma=False
     )

time: 145 us -> 139 us (0.959)
  local copies, waits for them, and re-layouts: 3.61 us -> 0 us
  Pallas kernels: 141 us -> 138 us
    pallas_call x1, Pallas kernels: 141 us -> 136 us  [per_device(): pl.pallas_call(body, out_shape=(jax.ShapeDtypeStruct((1, TICKS, HALF, D),...]
    unnamed x7 -> x0, local copies, waits for them, and re-layouts: 3.61 us -> none
    pallas_call x0 -> x1, Pallas kernels: none -> 2.01 us  [per_device(): pl.pallas_call(put, out_shape=tuple((jax.ShapeDtypeStruct(r.shape, r.dtyp...]
where the time goes in v3:
time: 139 us
  Pallas kernels  138 us (99%)
    pallas_call x1, Pallas kernels, per_device(): pl.pallas_call(body, out_shape=(jax.ShapeDtypeStruct((1, TICKS, HALF, D),...  136 us

profile of v3, /device:TPU:1, one launch (start us, length us, event | category | flops | bytes accessed | tf_op | source)
XLA Modules:
  0.0 139.1 jit_solution(2248503110824474468)
XLA Ops:
  0.6 136.4 %window.1 = (bf16[1,2,48,2048]{3,2,1,0:T(8,128)(2,1)}, bf16[1,2,48,2048]{3,2,1,0:T(8,128)(2,1)}, f32[1,512,128]{2,1,0:T(8,128)}) custom-call(bf16[2,96,2048]{2,1,0:T(8,128)(2,1)} %refs_0_.1, bf16[1,96,2048]{2,1,0:T(8,128)(2,1)} %refs_1_.1, bf16[2,96,2048]{2,1,0:T(8,128)(2,1)} %refs_2_.1, bf16[1,96,2048]{2,1,0:T(8,128)(2,1)} %refs_3_.1, ...), custom_call_target="tpu_custom_call" | custom-call | tf_op jit(solution)/shard_map/window/pallas_call | solution.py:691
  137.1 2.0 %put.1 = (bf16[1,2,48,2048]{3,2,1,0:T(8,128)(2,1)}, bf16[1,2,48,2048]{3,2,1,0:T(8,128)(2,1)}, f32[1,512,128]{2,1,0:T(8,128)}) custom-call(bf16[1,2,48,2048]{3,2,1,0:T(8,128)(2,1)} %get-tuple-element.6.refs_0_, bf16[1,2,48,2048]{3,2,1,0:T(8,128)(2,1)} %get-tuple-element.7.refs_1_, f32[1,512,128]{2,1,0:T(8,128)} %get-tuple-element.8.refs_2_), custom_call_target="tpu_custom_call" | custom-call | tf_op jit(solution)/shard_map/put/pallas_call | solution.py:719

commit v4 on v3

--- a/solution.py
+++ b/solution.py
@@ -6,7 +6,7 @@
 from jax.sharding import PartitionSpec as P
 
 HEAD = 128
-AHEAD_AFTER = 2
+AHEAD_AFTER = 0
 HEADS = 4
 WIDE = 4 * HEAD
 BLOCK = 24
@@ -553,9 +553,6 @@
             back_quarter(n - 1, nears[n - 1])
     back_quarter(PARTS - 1, nears[-1])
     a2a_pass(1)
-    dgat[...] = dgat_s[...].astype(BF16)
-    back_second(1, 0)
-    back_second(1, 1)
 
     finish_ring()
     a2a_wait(0)
@@ -575,6 +572,9 @@
         wsend[i] = wblock(peer_z[i]).astype(BF16)
         start(wcopy(i, z))
 
+    dgat[...] = dgat_s[...].astype(BF16)
+    back_second(1, 0)
+    back_second(1, 1)
     nears = [hand_on(0, 0, xin, ahead_far)]
     back_second(1, 2)
     nears.append(hand_on(0, 1, xin, ahead_far))

time: 139 us -> 143 us (1.029)
  the two profiles are of different devices: /device:TPU:1 before, /device:TPU:25 now
where the time goes in v4:
time: 143 us
  Pallas kernels  142 us (99%)
    pallas_call x1, Pallas kernels, per_device(): pl.pallas_call(body, out_shape=(jax.ShapeDtypeStruct((1, TICKS, HALF, D),...  140 us

profile of v4, /device:TPU:25, one launch (start us, length us, event | category | flops | bytes accessed | tf_op | source)
XLA Modules:
  0.0 142.5 jit_solution(13481754319891889614)
XLA Ops:
  0.6 139.9 %window.1 = (bf16[1,2,48,2048]{3,2,1,0:T(8,128)(2,1)}, bf16[1,2,48,2048]{3,2,1,0:T(8,128)(2,1)}, f32[1,512,128]{2,1,0:T(8,128)}) custom-call(bf16[2,96,2048]{2,1,0:T(8,128)(2,1)} %refs_0_.1, bf16[1,96,2048]{2,1,0:T(8,128)(2,1)} %refs_1_.1, bf16[2,96,2048]{2,1,0:T(8,128)(2,1)} %refs_2_.1, bf16[1,96,2048]{2,1,0:T(8,128)(2,1)} %refs_3_.1, ...), custom_call_target="tpu_custom_call" | custom-call | tf_op jit(solution)/shard_map/window/pallas_call | solution.py:691
  140.5 2.0 %put.1 = (bf16[1,2,48,2048]{3,2,1,0:T(8,128)(2,1)}, bf16[1,2,48,2048]{3,2,1,0:T(8,128)(2,1)}, f32[1,512,128]{2,1,0:T(8,128)}) custom-call(bf16[1,2,48,2048]{3,2,1,0:T(8,128)(2,1)} %get-tuple-element.6.refs_0_, bf16[1,2,48,2048]{3,2,1,0:T(8,128)(2,1)} %get-tuple-element.7.refs_1_, f32[1,512,128]{2,1,0:T(8,128)} %get-tuple-element.8.refs_2_), custom_call_target="tpu_custom_call" | custom-call | tf_op jit(solution)/shard_map/put/pallas_call | solution.py:719
